TPU v7x, 32 devices: a whole 2x2x4 slice. The times are simulated.
32 devices in a mesh: flux: 4 (over z), obs: 8 (over y, x, core).
Axes of the slice: x: 2, y: 2, z: 4, core: 2. Of those that a mesh axis runs over, the one named last changes fastest.
Arguments:
- footprint: bfloat16 [256, 4, 4, 2, 4096], P(('flux', 'obs')), may hold values from 0.00049972534 to 0.049804688
- obs_hour: int32 [256, 4], P(('flux', 'obs')), may hold values from 0 to 3
- tile_list: int32 [256, 4], P(('flux', 'obs')), may hold values from 0 to 511, as said below
- tile_row: int32 [512], replicated, may hold values from 0 to 511, as said below
- flux: bfloat16 [512, 5, 4096], P('flux'), may hold values from -6 to 6
- observed: float32 [256, 4], P(('flux', 'obs')), may hold values from -18 to 18
- obs_var: float32 [256, 4], P(('flux', 'obs')), may hold values from 0.5 to 4
Outputs:
- modeled: float32 [256, 4], P(('flux', 'obs'))
- gradient: float32 [512, 5, 4096], P('flux', None, 'obs')
Inputs may be any that keep to these rules, and one draw needn't show every extreme that they name: `tile_row`: A permutation: every tile has its own storage row, and the row r lies on index r // 128 of flux. `tile_list`: among the 32 listed tiles of one device's 8 blocks, at most 16 have storage rows on one index of flux; on every device some index of flux gets exactly 16.
All inputs are finite; a program needn't handle non-finite values.
Results may differ from a plain program's by a relative error of at most 0.0019.
Values may be sent and summed in bfloat16 or wider, within the bound.
No kernel may reach another device: no remote copies, remote signals or barrier semaphores. Data moves between devices by JAX's collectives and lax.ppermute only.
A program may use at most 64 MiB of HBM per device.

v0:
```python
import functools

import jax
import jax.numpy as jnp
from jax import lax
from jax.experimental import pallas as pl
from jax.experimental.pallas import tpu as pltpu
from jax.sharding import PartitionSpec as P

LANES = 128
VMEM_BYTES = 48 * 1024 * 1024
ALL_VMEM_BYTES = 60 * 1024 * 1024
BASE = 256
REST = (0, 64, 128)
PACK_STEPS = 2


def iota(shape, dim):
    return lax.broadcasted_iota(jnp.int32, shape, dim)


def thirds(value):
    high = value.astype(jnp.bfloat16).astype(jnp.float32)
    rest = value - high
    middle = rest.astype(jnp.bfloat16).astype(jnp.float32)
    return high, middle, (rest - middle).astype(jnp.bfloat16).astype(jnp.float32)


class Sizes:
    def __init__(self, owners, columns, footprint, flux):
        self.owners, self.columns = owners, columns
        self.devices = owners * columns
        self.blocks, self.width, self.soundings, self.lags, cells = footprint
        self.tiles, self.hours = flux[0], flux[1]
        self.span = self.hours - self.lags + 1
        self.half = self.span * self.tiles // 2
        self.slots = self.blocks * self.width
        self.per_slot = self.soundings * self.lags
        self.part = cells // columns
        self.lane_tiles = self.part // LANES
        capacity = 2 * self.slots // owners
        self.first = capacity // 2 - capacity // 16
        self.rows = self.first * self.per_slot
        self.spill = (self.slots - owners // 2 * self.first) * self.per_slot
        self.spill_notes = -(-self.spill // LANES)
        self.second = columns * (capacity - self.first) * self.per_slot
        self.base = min(BASE, self.second)
        self.rest = self.second - self.base
        self.base_notes = 8 * -(-self.base // self.part)
        self.rest_notes = 8 * -(-self.rest // self.part)
        self.levels = tuple(n for n in REST if n < self.rest) + (self.rest,)
        self.states = self.blocks * self.soundings
        self.per_page = 8 * LANES // self.states
        self.pages = self.devices // self.per_page


def read_notes(sizes, notes, plane):
    lane = iota((1, notes.shape[1]), 1)
    inner = lax.rem(lane, jnp.int32(sizes.per_slot))
    base = notes[0:1]
    target = (base + sizes.half).astype(jnp.int32) + lax.rem(inner, jnp.int32(sizes.lags)) * sizes.tiles
    target = jnp.where(base > sizes.half - 0.5, -1, target)
    place = notes[1:2].astype(jnp.int32)
    block = lax.rem(place, jnp.int32(sizes.blocks))
    device = plane * sizes.columns + lax.div(place, jnp.int32(sizes.blocks))
    state = block * sizes.soundings + lax.div(inner, jnp.int32(sizes.lags))
    row = lax.div(device, jnp.int32(sizes.per_page)) * 8 + lax.rem(state, jnp.int32(8))
    column = lax.div(state, jnp.int32(8)) * sizes.per_page + lax.rem(device, jnp.int32(sizes.per_page))
    seen = notes[2:3] + notes[3:4] + notes[4:5]
    spread = notes[5:6] + notes[6:7] + notes[7:8]
    places = [each.astype(jnp.float32) for each in (target, row, column)]
    return jnp.concatenate(places + [seen, spread, jnp.zeros((3, lane.shape[1]), jnp.float32)], axis=0)


def first_round(sizes, ref, step):
    sources, count = ref.shape[0], sizes.rows
    feet = jnp.concatenate(
        [
            ref[:, n * count : (n + 1) * count, :].reshape(sources * count, LANES)
            for n in range(sizes.lane_tiles)
        ],
        axis=1,
    )
    end = sizes.lane_tiles * count
    notes = jnp.concatenate(
        [ref[s, end : end + 8, :].astype(jnp.float32)[:, :count] for s in range(sources)], axis=1
    )
    lane = iota((1, sources * count), 1)
    plane = lax.div(step * sources + lax.div(lane, jnp.int32(count)), jnp.int32(sizes.columns))
    return feet, notes, plane


def second_round(sizes, flux_index, refs, first, heights, count):
    notes = [
        jnp.concatenate(
            [ref[n * 8 : (n + 1) * 8, :].astype(jnp.float32) for n in range(heights // 8)], axis=1
        )[:, :count]
        for ref in refs
    ]
    plane = first + lax.div(iota((1, len(refs) * count), 1), jnp.int32(count))
    feet = jnp.concatenate([ref[heights : heights + count, :] for ref in refs], axis=0)
    return feet, jnp.concatenate(notes, axis=1), lax.bitwise_xor(plane, flux_index)


def partial_sums(sizes, flux_ref, feet, read):
    target, row, column = (read[n : n + 1].astype(jnp.int32) for n in range(3))
    count = feet.shape[0]
    levels = sizes.hours * sizes.tiles
    products = lax.dot_general(
        flux_ref[...].reshape(levels, sizes.part),
        feet,
        (((1,), (1,)), ((), ())),
        preferred_element_type=jnp.float32,
    )
    chosen = jnp.where(iota((levels, count), 0) == target, products, 0.0)
    partial = jnp.sum(chosen, axis=0, keepdims=True)
    height = 8 * sizes.pages
    spread = jnp.where(iota((height, count), 0) == row, partial, 0.0)
    terms = jnp.concatenate(thirds(spread), axis=0).astype(jnp.bfloat16)
    lanes = (iota((LANES, count), 0) == column).astype(jnp.bfloat16)
    sums = lax.dot_general(
        terms, lanes, (((1,), (1,)), ((), ())), preferred_element_type=jnp.float32
    )
    return sums[:height] + sums[height : 2 * height] + sums[2 * height :]


def coefficients(sizes, model, read):
    target, row, column = (read[n : n + 1].astype(jnp.int32) for n in range(3))
    count = read.shape[1]
    height = 8 * sizes.pages
    lanes = (iota((LANES, count), 0) == column).astype(jnp.bfloat16)
    taken = jnp.dot(model, lanes, preferred_element_type=jnp.float32)
    taken = taken[:height] + taken[height : 2 * height] + taken[2 * height :]
    value = jnp.sum(
        jnp.where(iota((height, count), 0) == row, taken, 0.0), axis=0, keepdims=True
    )
    scaled = ((value - read[3:4]) / read[4:5]).astype(jnp.bfloat16).astype(jnp.float32)
    levels = sizes.hours * sizes.tiles
    return jnp.where(iota((levels, count), 0) == target, scaled, 0.0).astype(jnp.bfloat16)


def pack_kernel(sizes, at_ref, *refs):
    tables, feet_ref, send_ref = refs[:5], refs[5], refs[6]
    spills = refs[7 : 7 + sizes.columns]
    feet, sent, spilled, first_notes, count, *local = refs[7 + sizes.columns : -4]
    arrived, feet_arrived, sent_done, over_done = refs[-4:]
    list_ref, row_ref, hour_ref, seen_ref, var_ref = local
    owners, per_slot = sizes.owners, sizes.per_slot
    group = sizes.columns // PACK_STEPS
    mine = at_ref[1]
    tables = [
        pltpu.make_async_copy(table, here, arrived.at[n])
        for n, (table, here) in enumerate(zip(tables, local))
    ]
    for copy in tables:
        copy.start()
    firsts = [pl.multiple_of((i ^ (mine // group)) * group, group) for i in range(PACK_STEPS)]
    loads = []
    for i, first in enumerate(firsts):
        lanes = pl.ds(pl.multiple_of(first * sizes.part, LANES), group * sizes.part)
        loads.append(
            pltpu.make_async_copy(feet_ref.at[:, :, lanes], feet.at[i], feet_arrived.at[i])
        )
        loads[-1].start()
    for copy in tables:
        copy.wait()

    field, lane = iota((16, LANES), 0), iota((16, LANES), 1)
    inner = lane % per_slot
    sounding = inner // sizes.lags
    slot_at = lane // per_slot
    key_at = iota((1, sizes.slots * per_slot), 1)
    key = jnp.zeros(key_at.shape, jnp.int32)
    empty = jnp.where(field == 0, jnp.float32(sizes.half), 0.0)
    empty = jnp.where(field == 5, 1.0, jnp.where(field == 8, -1.0, empty))
    for o in range(owners):
        count[o] = 0
        first_notes[o] = empty[:8]
    count[owners] = 0
    lefts = [empty] * sizes.spill_notes
    for b in range(sizes.blocks):
        base = jnp.zeros(field.shape, jnp.float32)
        seen = jnp.zeros(field.shape, jnp.float32)
        spread = jnp.ones(field.shape, jnp.float32)
        for o in range(sizes.soundings):
            here = sounding == o
            hour = hour_ref[o, b] * sizes.tiles - sizes.half
            base = jnp.where(here, hour.astype(jnp.float32), base)
            seen = jnp.where(here, seen_ref[o, b], seen)
            spread = jnp.where(here, var_ref[o, b], spread)
        column = (b + sizes.blocks * at_ref[1]).astype(jnp.float32)
        pattern = jnp.where(field == 0, base, jnp.where(field == 1, column, 0.0))
        for n, term in enumerate(thirds(seen) + thirds(spread)):
            pattern = jnp.where(field == 2 + n, term, pattern)
        for k in range(sizes.width):
            stored = row_ref[list_ref[k, b]]
            owner = lax.div(stored, jnp.int32(sizes.tiles))
            tile = (stored - owner * sizes.tiles).astype(jnp.float32)
            position = count[owner]
            count[owner] = position + 1
            keep = position < sizes.first
            over = count[owners]
            count[owners] = over + jnp.where(keep, 0, 1)
            goes = jnp.where(
                keep, owner * sizes.first + position, owners * sizes.first + over
            )
            value = jnp.where(field == 0, pattern + tile, pattern)
            value = jnp.where(field == 8, owner.astype(jnp.float32), value)
            value = jnp.where(
                field == 9, (position - sizes.first).astype(jnp.float32), value
            )
            first_notes[owner] = jnp.where(
                slot_at[:8] == jnp.where(keep, position, -1), value[:8], first_notes[owner]
            )
            lefts = [
                jnp.where(
                    slot_at + n * (LANES // per_slot) == jnp.where(keep, -1, over), value, left
                )
                for n, left in enumerate(lefts)
            ]
            key = jnp.where(
                key_at // per_slot == b * sizes.width + k,
                goes * per_slot + key_at % per_slot,
                key,
            )
    counts = jnp.zeros((8, LANES), jnp.float32)
    for o in range(owners):
        over = jnp.maximum(count[o] - sizes.first, 0).astype(jnp.float32)
        counts = jnp.where(lane[:8] == sizes.rows + o, over, counts)
    for o in range(owners):
        first_notes[o] = jnp.where(lane[:8] < sizes.rows, first_notes[o], counts)
    place = (iota((owners * sizes.rows + sizes.spill, key.shape[1]), 0) == key).astype(
        jnp.bfloat16
    )
    rows, spill, tiles = sizes.rows, sizes.spill, sizes.lane_tiles
    end = tiles * rows
    stores = []
    for i, first in enumerate(firsts):
        loads[i].wait()
        packed = jnp.dot(
            place,
            feet[i].reshape(key.shape[1], group * sizes.part),
            preferred_element_type=jnp.float32,
        )
        for c in range(group):
            for o in range(owners):
                for n in range(tiles):
                    lanes = slice((c * tiles + n) * LANES, (c * tiles + n + 1) * LANES)
                    sent[i, o, c, n * rows : (n + 1) * rows, :] = packed[
                        o * rows : (o + 1) * rows, lanes
                    ].astype(jnp.bfloat16)
                sent[i, o, c, end : end + 8, :] = first_notes[o].astype(jnp.bfloat16)
            for n in range(tiles):
                lanes = slice((c * tiles + n) * LANES, (c * tiles + n + 1) * LANES)
                spilled[i, c, n * spill : (n + 1) * spill, :] = packed[
                    owners * rows :, lanes
                ].astype(jnp.bfloat16)
            for n, left in enumerate(lefts):
                first_note = tiles * spill + n * 16
                spilled[i, c, first_note : first_note + 16, :] = left.astype(jnp.bfloat16)
        stores.append(
            pltpu.make_async_copy(
                sent.at[i], send_ref.at[:, pl.ds(first, group)], sent_done.at[i]
            )
        )
        stores[-1].start()
        for d in range(i * group, (i + 1) * group):
            stores.append(
                pltpu.make_async_copy(spilled.at[i, (d ^ mine) % group], spills[d], over_done.at[d])
            )
            stores[-1].start()
    for copy in stores:
        copy.wait()


def level_of(sizes, ref):
    planes = [
        sum(
            ref[p * sizes.columns + j].astype(jnp.float32) for j in range(sizes.columns)
        )
        for p in range(sizes.owners)
    ]
    counts = functools.reduce(jnp.maximum, planes)[0:1]
    lane = iota(counts.shape, 1)
    counts = jnp.where((lane >= sizes.rows) & (lane < sizes.rows + sizes.owners), counts, 0.0)
    most = jnp.max(counts, axis=1, keepdims=True) * sizes.per_slot
    level = jnp.zeros((1, 1), jnp.int32)
    for n in sizes.levels[:-1]:
        level = level + jnp.where(most > sizes.base + n, 1, 0)
    return level


def regroup_kernel(sizes, start, count, heights, at_ref, *refs):
    columns, owners, spill = sizes.columns, sizes.owners, sizes.spill
    spills, outs, (feet,) = refs[:columns], refs[columns : columns + owners], refs[-1:]
    end = sizes.lane_tiles * spill
    notes = []
    for d, ref in enumerate(spills):
        for n in range(sizes.lane_tiles):
            feet[d * spill : (d + 1) * spill, n * LANES : (n + 1) * LANES] = ref[
                n * spill : (n + 1) * spill, :
            ]
        blocks = [
            ref[end + n * 16 : end + (n + 1) * 16, :].astype(jnp.float32)
            for n in range(sizes.spill_notes)
        ]
        notes.append(jnp.concatenate(blocks, axis=1)[:, :spill])
    owner_at = jnp.concatenate([each[8:9] for each in notes], axis=0)
    position = jnp.concatenate([each[9:10] for each in notes], axis=0).astype(jnp.int32)
    inner = lax.rem(iota(position.shape, 1), jnp.int32(sizes.per_slot))
    fields = jnp.concatenate([each[0:8] for each in notes], axis=1).astype(jnp.bfloat16)
    for n in range(owners):
        mine = owner_at == (at_ref[2] ^ n).astype(jnp.float32)
        counts = jnp.sum(jnp.where(mine, 1.0, 0.0), axis=1, keepdims=True).astype(jnp.int32)
        keys, total = [], jnp.zeros((1, 1), jnp.int32)
        for d in range(columns):
            row = total + position[d : d + 1] * sizes.per_slot + inner[d : d + 1] - start
            keys.append(jnp.where(mine[d : d + 1], row, -1))
            total = total + counts[d : d + 1]
        key = jnp.concatenate(keys, axis=1)
        place = (iota((count, columns * spill), 0) == key).astype(jnp.bfloat16)
        outs[n][heights:, :] = jnp.dot(
            place, feet[...], preferred_element_type=jnp.float32
        ).astype(jnp.bfloat16)
        moved = lax.dot_general(
            fields, place, (((1,), (1,)), ((), ())), preferred_element_type=jnp.float32
        )
        field, lane = iota(moved.shape, 0), iota(moved.shape, 1)
        empty = jnp.where(field == 0, jnp.float32(sizes.half), jnp.where(field == 5, 1.0, 0.0))
        moved = jnp.where(lane + start < total, moved, empty)
        for m in range(heights // 8):
            lanes = moved[:, m * sizes.part : (m + 1) * sizes.part].astype(jnp.bfloat16)
            outs[n][m * 8 : (m + 1) * 8, : lanes.shape[1]] = lanes


def forward_first_kernel(
    sizes, at_ref, flux_ref, got_ref, all_ref, out_ref, level_ref, feet_ref, read_ref
):
    step = pl.program_id(0)
    feet, notes, plane = first_round(sizes, got_ref, step)
    read = read_notes(sizes, notes, plane)
    feet_ref[...], read_ref[...] = feet, read
    sums = partial_sums(sizes, flux_ref, feet, read)

    @pl.when(step == 0)
    def _():
        out_ref[...] = sums
        level_ref[...] = jnp.broadcast_to(level_of(sizes, all_ref), level_ref.shape)

    @pl.when(step > 0)
    def _():
        out_ref[...] += sums


def forward_second_kernel(sizes, first, heights, count, at_ref, flux_ref, before_ref, *refs):
    *parts, out_ref, read_ref = refs
    feet, notes, plane = second_round(sizes, at_ref[2], parts, first, heights, count)
    read = read_notes(sizes, notes, plane)
    read_ref[...] = read
    sums = before_ref[0] + partial_sums(sizes, flux_ref, feet, read)
    out_ref[...] = jnp.broadcast_to(sums[None], out_ref.shape)


def adjoint_kernel(
    sizes, more, at_ref, sums_ref, feet_ref, read_ref, read_second_ref, read_last_ref, *refs
):
    bases, rests = refs[: sizes.owners], refs[sizes.owners : -4]
    modeled_ref, out_ref, grad_ref, written = refs[-4:]
    sums = jnp.sum(sums_ref[...], axis=0)
    model = jnp.concatenate(thirds(sums), axis=0).astype(jnp.bfloat16)
    me = at_ref[0]
    page, within = lax.div(me, sizes.per_page), lax.rem(me, sizes.per_page)
    lane = iota((8, LANES), 1)
    own = jnp.zeros((8, LANES), jnp.float32)
    for p in range(sizes.pages):
        own = jnp.where(page == p, sums[p * 8 : (p + 1) * 8], own)
    result = jnp.zeros(modeled_ref.shape, jnp.float32)
    at_block = iota(modeled_ref.shape, 1)
    each = 8 // sizes.soundings
    for q in range(sizes.states // 8):
        picked = jnp.where(lane == q * sizes.per_page + within, own, 0.0)
        column = jnp.sum(picked, axis=1, keepdims=True)
        for n in range(each):
            values = column[n * sizes.soundings : (n + 1) * sizes.soundings]
            result = jnp.where(at_block == q * each + n, values, result)
    modeled_ref[...] = result

    pairs = [(coefficients(sizes, model, read_ref[...]), feet_ref, 0, feet_ref.shape[0])]
    reads = jnp.concatenate([read_second_ref[...], read_last_ref[...]], axis=1)
    second = coefficients(sizes, model, reads)
    for n, ref in enumerate(bases):
        pairs.append(
            (second[:, n * sizes.base : (n + 1) * sizes.base], ref, sizes.base_notes, sizes.base)
        )
    if rests:
        *rests, read_more_ref = rests
        last = coefficients(sizes, model, read_more_ref[...])
        for n, ref in enumerate(rests):
            pairs.append((last[:, n * more : (n + 1) * more], ref, sizes.rest_notes, more))
    half = sizes.part // 2 if sizes.part > LANES else sizes.part
    copies = []
    for n in range(sizes.part // half):
        lanes = slice(n * half, (n + 1) * half)
        terms = sum(
            jnp.dot(each, ref[first : first + count, lanes], preferred_element_type=jnp.float32)
            for each, ref, first, count in pairs
        )
        grad_ref[:, :, lanes] = terms.reshape(sizes.hours, sizes.tiles, half)
        copies.append(
            pltpu.make_async_copy(grad_ref.at[:, :, lanes], out_ref.at[:, :, lanes], written.at[n])
        )
        copies[-1].start()
    for copy in copies:
        copy.wait()


def shards(footprint, obs_hour, tile_list, tile_row, flux, observed, obs_var):
    sizes = Sizes(
        lax.axis_size("flux"), lax.axis_size("obs"), footprint.shape, flux.shape
    )
    owners, columns, devices, part = sizes.owners, sizes.columns, sizes.devices, sizes.part
    both = ("flux", "obs")
    params = pltpu.CompilerParams(vmem_limit_bytes=VMEM_BYTES)
    me = lax.axis_index("flux") * columns + lax.axis_index("obs")
    at = jnp.stack([me, lax.axis_index("obs"), lax.axis_index("flux")])
    flux = flux.transpose(1, 0, 2)

    first_height = sizes.lane_tiles * sizes.rows + 8
    spill_height = sizes.lane_tiles * sizes.spill + sizes.spill_notes * 16
    all_slots = sizes.slots * sizes.per_slot
    group = columns // PACK_STEPS
    tables = (tile_list.T, tile_row, obs_hour.T, observed.T, obs_var.T)
    send, *spills = pl.pallas_call(
        functools.partial(pack_kernel, sizes),
        in_specs=[pl.BlockSpec(memory_space=pltpu.SMEM)]
        + [pl.BlockSpec(memory_space=pltpu.HBM)] * 6,
        out_specs=[pl.BlockSpec(memory_space=pltpu.HBM)] * (1 + columns),
        scratch_shapes=[
            pltpu.VMEM(
                (PACK_STEPS, all_slots // sizes.lags, sizes.lags, group * part), jnp.bfloat16
            ),
            pltpu.VMEM((PACK_STEPS, owners, group, first_height, LANES), jnp.bfloat16),
            pltpu.VMEM((PACK_STEPS, group, spill_height, LANES), jnp.bfloat16),
            pltpu.VMEM((owners, 8, LANES), jnp.float32),
            pltpu.SMEM((owners + 1,), jnp.int32),
        ]
        + [pltpu.SMEM(table.shape, table.dtype) for table in tables]
        + [pltpu.SemaphoreType.DMA((n,)) for n in (5, PACK_STEPS, PACK_STEPS, columns)],
        out_shape=[pltpu.HBM((owners, columns, first_height, LANES), jnp.bfloat16)]
        + [jax.ShapeDtypeStruct((spill_height, LANES), jnp.bfloat16)] * columns,
        compiler_params=pltpu.CompilerParams(vmem_limit_bytes=ALL_VMEM_BYTES),
        name="pack",
    )(
        at,
        *tables,
        footprint.reshape(all_slots // sizes.lags, sizes.lags, columns * part),
    )
    got = lax.all_to_all(
        send.reshape(devices, first_height, LANES), both, split_axis=0, concat_axis=0, tiled=True
    )
    mine = spills[0]
    spills = spills[:1] + [
        lax.ppermute(spills[d], "obs", [(i, i ^ d) for i in range(columns)])
        for d in range(1, columns)
    ]
    smem, vmem = pl.BlockSpec(memory_space=pltpu.SMEM), pl.BlockSpec(memory_space=pltpu.VMEM)

    def regroup(spills, start, count, heights, name):
        shape = jax.ShapeDtypeStruct((heights + count, part), jnp.bfloat16)
        return pl.pallas_call(
            functools.partial(regroup_kernel, sizes, start, count, heights),
            in_specs=[smem] + [vmem] * columns,
            out_specs=[vmem] * owners,
            out_shape=[shape] * owners,
            scratch_shapes=[pltpu.VMEM((columns * sizes.spill, part), jnp.bfloat16)],
            compiler_params=params,
            name=name,
        )(at, *spills)

    def swap(arrays):
        return arrays[:1] + [
            lax.ppermute(arrays[n], "flux", [(i, i ^ n) for i in range(owners)])
            for n in range(1, owners)
        ]

    bases = swap(list(regroup(spills, 0, sizes.base, sizes.base_notes, "regroup")))

    sources = min(devices, 1 << (1024 // sizes.rows).bit_length() - 1)
    chunks = devices // sources
    copies = devices if devices <= 64 else 1
    height = 8 * sizes.pages
    flux_spec = pl.BlockSpec((sizes.hours, sizes.tiles, part), lambda i, at: (0, 0, at[1]))
    early, level, feet_first, read_first = pl.pallas_call(
        functools.partial(forward_first_kernel, sizes),
        grid_spec=pltpu.PrefetchScalarGridSpec(
            num_scalar_prefetch=1,
            grid=(chunks,),
            in_specs=[
                flux_spec,
                pl.BlockSpec((sources, first_height, LANES), lambda i, at: (i, 0, 0)),
                pl.BlockSpec((devices, 8, LANES), lambda i, at: (0, first_height // 8 - 1, 0)),
            ],
            out_specs=(
                pl.BlockSpec((height, LANES), lambda i, at: (0, 0)),
                pl.BlockSpec((8, LANES), lambda i, at: (0, 0)),
                pl.BlockSpec((sources * sizes.rows, part), lambda i, at: (i, 0)),
                pl.BlockSpec((8, sources * sizes.rows), lambda i, at: (0, i)),
            ),
        ),
        out_shape=(
            jax.ShapeDtypeStruct((height, LANES), jnp.float32),
            jax.ShapeDtypeStruct((8, LANES), jnp.int32),
            jax.ShapeDtypeStruct((devices * sizes.rows, part), jnp.bfloat16),
            jax.ShapeDtypeStruct((8, devices * sizes.rows), jnp.float32),
        ),
        compiler_params=params,
        name="forward_first",
    )(at, flux, got, got)

    late_flux = lax.optimization_barrier((flux, mine))[0]
    own_flux = lax.dynamic_slice_in_dim(late_flux, lax.axis_index("obs") * part, part, axis=2)

    def forward_second(own_flux, before, parts, first, heights, count, name):
        return pl.pallas_call(
            functools.partial(forward_second_kernel, sizes, first, heights, count),
            in_specs=[smem] + [vmem] * (2 + len(parts)),
            out_specs=(vmem, vmem),
            out_shape=(
                jax.ShapeDtypeStruct((copies, height, LANES), jnp.float32),
                jax.ShapeDtypeStruct((8, len(parts) * count), jnp.float32),
            ),
            compiler_params=params,
            name=name,
        )(at, own_flux, before, *parts)

    late_spills = lax.optimization_barrier((spills, early))[0]
    rests = list(regroup(late_spills, sizes.base, sizes.rest, sizes.rest_notes, "regroup_rest"))

    def follow(more):
        def run(rests):
            height, results, before = sizes.rest_notes + more, rests[:1], ()
            for n in range(1, owners):
                rest = lax.optimization_barrier((rests[n][:height], before))[0]
                before = lax.ppermute(rest, "flux", [(i, i ^ n) for i in range(owners)])
                results.append(lax.dynamic_update_slice(rests[n], before, (0, 0)))
            return results

        return run if more else lambda rests: rests

    level = level[0, 0]
    rests = lax.switch(level, [follow(n) for n in sizes.levels], rests)

    reads = []
    sums = early[None]
    for first, end in ((0, owners - 1), (owners - 1, owners)):
        sums, read = forward_second(
            own_flux, sums, bases[first:end], first, sizes.base_notes, sizes.base, "forward_second"
        )
        reads.append(read)
    kept = (feet_first, read_first, *reads)

    def finish(more):
        def run(own_flux, kept, sums, bases, rests, at):
            if more:
                sums, read_more = forward_second(
                    own_flux, sums, rests, 0, sizes.rest_notes, more, "forward_more"
                )
                rests = rests + [read_more]
            else:
                rests = []
            if copies > 1:
                sums = lax.all_to_all(sums, both, split_axis=0, concat_axis=0, tiled=True)
            else:
                sums = lax.psum(sums, both)
            return pl.pallas_call(
                functools.partial(adjoint_kernel, sizes, more),
                in_specs=[smem] + [vmem] * (5 + len(bases) + len(rests)),
                out_specs=(vmem, pl.BlockSpec(memory_space=pltpu.HBM)),
                out_shape=(
                    jax.ShapeDtypeStruct((sizes.soundings, sizes.blocks), jnp.float32),
                    jax.ShapeDtypeStruct((sizes.hours, sizes.tiles, part), jnp.float32),
                ),
                scratch_shapes=[
                    pltpu.VMEM((sizes.hours, sizes.tiles, part), jnp.float32),
                    pltpu.SemaphoreType.DMA((2,)),
                ],
                compiler_params=params,
                name="adjoint",
            )(at, sums, *kept, *bases, *rests)

        return run

    modeled, gradient = lax.switch(
        level, [finish(n) for n in sizes.levels], own_flux, kept, sums, bases, rests, at
    )
    return modeled.T, gradient.transpose(1, 0, 2)


def solution(mesh):
    placed = (
        P(("flux", "obs"), None, None, None, None),
        P(("flux", "obs"), None),
        P(("flux", "obs"), None),
        P(),
        P("flux", None, None),
        P(("flux", "obs"), None),
        P(("flux", "obs"), None),
    )
    return jax.shard_map(
        shards,
        mesh=mesh,
        in_specs=placed,
        out_specs=(P(("flux", "obs"), None), P("flux", None, "obs")),
        check_vma=False,
    )
```

profile of v0, /device:TPU:0, one launch (start us, length us, event | category | flops | bytes accessed | tf_op | source)
XLA Modules:
  0.0 98.4 jit_solution(11711616538249771701)
XLA Ops:
  0.6 0.1 pad_add_fusion.at_ref
  0.7 4.2 %pack.1 = (bf16[4,8,232,128]{3,2,1,0:T(8,128)(2,1)}, bf16[608,128]{1,0:T(8,128)(2,1)}, bf16[608,128]{1,0:T(8,128)(2,1)}, bf16[608,128]{1,0:T(8,128)(2,1)}, bf16[...) custom-call(s32[3]{0:T(128)S(1)} %pad_add_fusion.at_ref, ...), custom_call_target="tpu_custom_call" | custom-call | tf_op jit(solution)/shard_map/pack/pallas_call | solution.py:433
  4.9 0.0 copy-start.8
  4.9 0.0 copy-start.7
  4.9 0.0 copy-start.6
  4.9 0.0 copy-start.5
  4.9 0.0 copy-start
  5.0 7.3 %all-to-all-start.4 = ((bf16[32,232,128]{2,1,0:T(8,128)(2,1)}), bf16[32,232,128]{2,1,0:T(8,128)(2,1)S(1)}, u32[]{:S(2)}, u32[]{:S(2)}) async-start(bf16[32,232,128]{2,1,0:T(8,128)(2,1)} %bitcast.18), calls=%async_computation.4 | async-start | bytes 3801088 | tf_op jit(solution)/shard_map/all_to_all | solution.py:458
  12.3 0.0 copy-done.8
  12.3 0.3 collective-permute-start.9
  12.6 0.0 copy-done.7
  12.6 1.7 %collective-permute-start.10 = (bf16[608,128]{1,0:T(8,128)(2,1)S(1)}, bf16[608,128]{1,0:T(8,128)(2,1)S(1)}, u32[]{:S(2)}, u32[]{:S(2)}) collective-permute-start(bf16[608,128]{1,0:T(8,128)(2,1)S(1)} %copy-done.7), channel_id=1, source_target_pairs={{0,2},{1,3},{2,0},{3,1},{4,6},{5,7},{6,4},{7,5},{8,10},{9,11},{10,... | collective-permute-start | bytes 466952 | tf_op jit(solution)/shard_map/ppermute | solution.py:463
  14.3 0.0 collective-permute-start.11
  14.3 1.7 %collective-permute-start.12 = (bf16[608,128]{1,0:T(8,128)(2,1)}, bf16[608,128]{1,0:T(8,128)(2,1)S(1)}, u32[]{:S(2)}, u32[]{:S(2)}) collective-permute-start(bf16[608,128]{1,0:T(8,128)(2,1)} %get-tuple-element.259), channel_id=1, source_target_pairs={{0,4},{1,5},{2,6},{3,7},{4,0},{5,1},{6,2},{7,3},{8,12},{9,13},{10,... | collective-permute-start | bytes 466952 | tf_op jit(solution)/shard_map/ppermute | solution.py:463
  16.0 0.1 collective-permute-start.13
  16.1 0.0 collective-permute-done.9.refs_1_
  16.1 0.0 copy-done.6
  16.1 2.6 %collective-permute-start.14 = (bf16[608,128]{1,0:T(8,128)(2,1)S(1)}, bf16[608,128]{1,0:T(8,128)(2,1)S(1)}, u32[]{:S(2)}, u32[]{:S(2)}) collective-permute-start(bf16[608,128]{1,0:T(8,128)(2,1)S(1)} %copy-done.6), channel_id=1, source_target_pairs={{0,6},{1,7},{2,4},{3,5},{4,2},{5,3},{6,0},{7,1},{8,14},{9,15},{10,... | collective-permute-start | bytes 466952 | tf_op jit(solution)/shard_map/ppermute | solution.py:463
  18.7 12.4 %collective-permute-done.10.refs_2_ = bf16[608,128]{1,0:T(8,128)(2,1)S(1)} collective-permute-done((bf16[608,128]{1,0:T(8,128)(2,1)S(1)}, bf16[608,128]{1,0:T(8,128)(2,1)S(1)}, u32[]{:S(2)}, u32[]{:S(2)}) %collective-permute-start.10) | collective-permute-done | bytes 155680 | tf_op jit(solution)/shard_map/ppermute | solution.py:463
  31.0 0.0 copy-done.5
  31.0 0.4 collective-permute-start.15
  31.4 6.4 %collective-permute-done.11.refs_3_ = bf16[608,128]{1,0:T(8,128)(2,1)S(1)} collective-permute-done((bf16[608,128]{1,0:T(8,128)(2,1)}, bf16[608,128]{1,0:T(8,128)(2,1)S(1)}, u32[]{:S(2)}, u32[]{:S(2)}) %collective-permute-start.11) | collective-permute-done | bytes 155680 | tf_op jit(solution)/shard_map/ppermute | solution.py:463
  37.8 0.0 collective-permute-done.12.refs_4_
  37.8 0.0 collective-permute-done.13.refs_5_
  37.8 6.3 %collective-permute-done.14.refs_6_ = bf16[608,128]{1,0:T(8,128)(2,1)S(1)} collective-permute-done((bf16[608,128]{1,0:T(8,128)(2,1)S(1)}, bf16[608,128]{1,0:T(8,128)(2,1)S(1)}, u32[]{:S(2)}, u32[]{:S(2)}) %collective-permute-start.14) | collective-permute-done | bytes 155680 | tf_op jit(solution)/shard_map/ppermute | solution.py:463
  44.1 2.7 %collective-permute-done.15.refs_7_ = bf16[608,128]{1,0:T(8,128)(2,1)S(1)} collective-permute-done((bf16[608,128]{1,0:T(8,128)(2,1)S(1)}, bf16[608,128]{1,0:T(8,128)(2,1)S(1)}, u32[]{:S(2)}, u32[]{:S(2)}) %collective-permute-start.15) | collective-permute-done | bytes 155680 | tf_op jit(solution)/shard_map/ppermute | solution.py:463
  46.8 0.0 copy-done
  46.8 3.2 %regroup.1 = (bf16[264,512]{1,0:T(8,128)(2,1)}, bf16[264,512]{1,0:T(8,128)(2,1)}, bf16[264,512]{1,0:T(8,128)(2,1)}, bf16[264,512]{1,0:T(8,128)(2,1)S(1)}) custom-call(s32[3]{0:T(128)S(1)} %pad_add_fusion.at_ref, bf16[608,128]{1,0:T(8,128)(2,1)S(1)} %copy-done, bf16[608,128]{1,0:T(8,128)(2,1)S(1)} %collective-permute-done.9.refs_1_, ...), custom_call_target="tpu_custom_call" | custom-call | tf_op jit(solution)/shard_map/regroup/pallas_call | solution.py:470
  50.0 3.3 %collective-permute-start.16 = (bf16[264,512]{1,0:T(8,128)(2,1)}, bf16[264,512]{1,0:T(8,128)(2,1)}, u32[]{:S(2)}, u32[]{:S(2)}) collective-permute-start(bf16[264,512]{1,0:T(8,128)(2,1)} %get-tuple-element.264), channel_id=1, source_target_pairs={{0,8},{8,0},{16,24},{24,16},{1,9},{9,1},{17,25},{25,17},{2,10},{10... | collective-permute-start | bytes 811016 | tf_op jit(solution)/shard_map/ppermute | solution.py:482
  53.3 1.8 %collective-permute-start.17 = (bf16[264,512]{1,0:T(8,128)(2,1)}, bf16[264,512]{1,0:T(8,128)(2,1)}, u32[]{:S(2)}, u32[]{:S(2)}) collective-permute-start(bf16[264,512]{1,0:T(8,128)(2,1)} %get-tuple-element.265), channel_id=1, source_target_pairs={{0,16},{8,24},{16,0},{24,8},{1,17},{9,25},{17,1},{25,9},{2,18},{10... | collective-permute-start | bytes 811016 | tf_op jit(solution)/shard_map/ppermute | solution.py:482
  55.1 0.6 collective-permute-start.18
  55.7 2.0 %constant_dynamic-slice_fusion.flux_ref = bf16[5,128,512]{2,1,0:T(8,128)(2,1)} fusion(bf16[5,128,4096]{2,1,0:T(8,128)(2,1)} %bitcast.15, s32[]{:T(128)S(6)} %select_n.3), kind=kLoop, calls=%fused_computation.7 | loop fusion | bytes 1310724 | tf_op jit(solution)/shard_map/dynamic_slice | solution.py:521
  57.7 0.0 all-to-all-done.4.got_ref.all_ref
  57.7 4.8 %forward_first.1 = (f32[8,128]{1,0:T(8,128)S(1)}, s32[8,128]{1,0:T(8,128)S(1)}, bf16[1792,512]{1,0:T(8,128)(2,1)}, f32[8,1792]{1,0:T(8,128)S(1)}) custom-call(s32[3]{0:T(128)S(1)} %pad_add_fusion.at_ref, bf16[5,128,4096]{2,1,0:T(8,128)(2,1)} %bitcast.16, bf16[32,232,128]{2,1,0:T(8,128)(2,1)S(1)} %all-to-all-done.4.got_ref.all_ref, ...), custom_call_target="tpu_custom_call" | custom-call | tf_op jit(solution)/shard_map/forward_first/pallas_call | solution.py:493
  62.5 0.5 slice.21
  63.6 4.1 %regroup_rest.1 = (bf16[328,512]{1,0:T(8,128)(2,1)}, bf16[328,512]{1,0:T(8,128)(2,1)}, bf16[328,512]{1,0:T(8,128)(2,1)}, bf16[328,512]{1,0:T(8,128)(2,1)}) custom-call(s32[3]{0:T(128)S(1)} %pad_add_fusion.at_ref, bf16[608,128]{1,0:T(8,128)(2,1)S(1)} %copy-done, bf16[608,128]{1,0:T(8,128)(2,1)S(1)} %collective-permute-done.9.refs_1_, ...), custom_call_target="tpu_custom_call" | custom-call | tf_op jit(solution)/shard_map/regroup_rest/pallas_call | solution.py:470
  67.7 0.0 copy-start.2
  67.7 0.0 copy-start.4
  67.7 0.0 copy-start.1
  67.7 0.0 copy-start.3
  67.7 0.0 collective-permute-done.16.refs_1_
  67.8 7.7 %collective-permute-done.17.refs_2_ = bf16[264,512]{1,0:T(8,128)(2,1)} collective-permute-done((bf16[264,512]{1,0:T(8,128)(2,1)}, bf16[264,512]{1,0:T(8,128)(2,1)}, u32[]{:S(2)}, u32[]{:S(2)}) %collective-permute-start.17) | collective-permute-done | bytes 270368 | tf_op jit(solution)/shard_map/ppermute | solution.py:482
  75.5 0.0 copy-done.2
  75.5 0.0 copy-done.4
  75.5 2.0 %forward_second.2 = (f32[32,8,128]{2,1,0:T(8,128)S(1)}, f32[8,768]{1,0:T(8,128)S(1)}) custom-call(s32[3]{0:T(128)S(1)} %pad_add_fusion.at_ref, bf16[5,128,512]{2,1,0:T(8,128)(2,1)S(1)} %copy-done.2, f32[1,8,128]{2,1,0:T(8,128)S(1)} %bitcast.14, bf16[264,512]{1,0:T(8,128)(2,1)S(1)} %copy-done.4, bf16[264,512]{1,0:T(8,128)(2,1)} %collective-permute-done.16.refs_1_, ...), custom_call_target="tpu_custom_call" | custom-call | tf_op jit(solution)/shard_map/forward_second/pallas_call | solution.py:524
  77.5 0.0 collective-permute-done.18.refs_0_
  77.5 1.6 %forward_second.3 = (f32[32,8,128]{2,1,0:T(8,128)S(1)}, f32[8,256]{1,0:T(8,128)S(1)}) custom-call(s32[3]{0:T(128)S(1)} %pad_add_fusion.at_ref, bf16[5,128,512]{2,1,0:T(8,128)(2,1)S(1)} %copy-done.2, f32[32,8,128]{2,1,0:T(8,128)S(1)} %get-tuple-element.266.before_ref, bf16[264,512]{1,0:T(8,128)(2,1)} %collective-permute-done.18.refs_0_), custom_call_target="tpu_custom_call" | custom-call | tf_op jit(solution)/shard_map/forward_second/pallas_call | solution.py:524
  79.1 0.0 copy-done.1
  79.1 0.0 copy-done.3
  79.1 19.1 %conditional.3 = ((f32[4,8]{1,0:T(4,128)}, f32[5,128,512]{2,1,0:T(8,128)})) conditional(s32[]{:T(128)} %bitcast.10, (f32[32,8,128]{2,1,0:T(8,128)S(1)}, s32[3]{0:T(128)S(1)}, bf16[1792,512]{1,0:T(8,128)(2,1)S(1)}, f32[8,1792]{1,0:T(8,128)S(1)}, f32[8,768]{1,0:T(8,128)S(1)}, /*index=5*/f32[8,256]{1,0:T(8,128)S(1)}, ...), branch_computations={%region_4.0_spmd, %region_5.0_spmd, %region_6.0_spmd, %region_7.0_... | conditional | bytes 262152 | solution.py:593
  79.1 13.9 %all_to_all.21.sums_ref = f32[32,8,128]{2,1,0:T(8,128)S(1)} all-to-all(f32[32,8,128]{2,1,0:T(8,128)S(1)} %get-tuple-element.150), channel_id=1, replica_groups=mesh['flux'=4,'obs'=8] {'flux','obs'}, dimensions={0} | all-to-all | bytes 262144 | tf_op jit(solution)/shard_map/cond/branch_0_fun/all_to_all | solution.py:572
  93.0 5.0 %adjoint.4 = (f32[4,8]{1,0:T(4,128)}, f32[5,128,512]{2,1,0:T(8,128)}) custom-call(s32[3]{0:T(128)S(1)} %get-tuple-element.149.at_ref, f32[32,8,128]{2,1,0:T(8,128)S(1)} %all_to_all.21.sums_ref, bf16[1792,512]{1,0:T(8,128)(2,1)S(1)} %get-tuple-element.151.feet_ref, f32[8,1792]{1,0:T(8,128)S(1)} %get-tuple-element.152.read_ref, ...), custom_call_target="tpu_custom_call" | custom-call | tf_op jit(solution)/shard_map/cond/branch_0_fun/adjoint/pallas_call | solution.py:575
  (1 shorter events, 0.0 us)
Async XLA Ops:
  4.9 7.4 %copy-start.8 = (bf16[608,128]{1,0:T(8,128)(2,1)S(1)}, bf16[608,128]{1,0:T(8,128)(2,1)}, u32[]{:S(2)}) copy-start(bf16[608,128]{1,0:T(8,128)(2,1)} %get-tuple-element.256) | copy-start | bytes 466948
  4.9 7.7 %copy-start.7 = (bf16[608,128]{1,0:T(8,128)(2,1)S(1)}, bf16[608,128]{1,0:T(8,128)(2,1)}, u32[]{:S(2)}) copy-start(bf16[608,128]{1,0:T(8,128)(2,1)} %get-tuple-element.257) | copy-start | bytes 466948
  4.9 11.2 %copy-start.6 = (bf16[608,128]{1,0:T(8,128)(2,1)S(1)}, bf16[608,128]{1,0:T(8,128)(2,1)}, u32[]{:S(2)}) copy-start(bf16[608,128]{1,0:T(8,128)(2,1)} %get-tuple-element.261) | copy-start | bytes 466948
  4.9 26.1 %copy-start.5 = (bf16[608,128]{1,0:T(8,128)(2,1)S(1)}, bf16[608,128]{1,0:T(8,128)(2,1)}, u32[]{:S(2)}) copy-start(bf16[608,128]{1,0:T(8,128)(2,1)} %get-tuple-element.262) | copy-start | bytes 466948
  4.9 41.9 %copy-start = (bf16[608,128]{1,0:T(8,128)(2,1)S(1)}, bf16[608,128]{1,0:T(8,128)(2,1)}, u32[]{:S(2)}) copy-start(bf16[608,128]{1,0:T(8,128)(2,1)} %get-tuple-element.273.refs_0_) | copy-start | bytes 466948
  5.0 52.7 %all-to-all-start.4 = ((bf16[32,232,128]{2,1,0:T(8,128)(2,1)}), bf16[32,232,128]{2,1,0:T(8,128)(2,1)S(1)}, u32[]{:S(2)}, u32[]{:S(2)}) async-start(bf16[32,232,128]{2,1,0:T(8,128)(2,1)} %bitcast.18), calls=%async_computation.4 | async-start | bytes 3801088 | tf_op jit(solution)/shard_map/all_to_all | solution.py:458
  12.3 3.8 %collective-permute-start.9 = (bf16[608,128]{1,0:T(8,128)(2,1)S(1)}, bf16[608,128]{1,0:T(8,128)(2,1)S(1)}, u32[]{:S(2)}, u32[]{:S(2)}) collective-permute-start(bf16[608,128]{1,0:T(8,128)(2,1)S(1)} %copy-done.8), channel_id=1, source_target_pairs={{0,1},{1,0},{2,3},{3,2},{4,5},{5,4},{6,7},{7,6},{8,9},{9,8},{10,11... | collective-permute-start | bytes 466952 | tf_op jit(solution)/shard_map/ppermute | solution.py:463
  12.6 18.5 %collective-permute-start.10 = (bf16[608,128]{1,0:T(8,128)(2,1)S(1)}, bf16[608,128]{1,0:T(8,128)(2,1)S(1)}, u32[]{:S(2)}, u32[]{:S(2)}) collective-permute-start(bf16[608,128]{1,0:T(8,128)(2,1)S(1)} %copy-done.7), channel_id=1, source_target_pairs={{0,2},{1,3},{2,0},{3,1},{4,6},{5,7},{6,4},{7,5},{8,10},{9,11},{10,... | collective-permute-start | bytes 466952 | tf_op jit(solution)/shard_map/ppermute | solution.py:463
  14.3 23.6 %collective-permute-start.11 = (bf16[608,128]{1,0:T(8,128)(2,1)}, bf16[608,128]{1,0:T(8,128)(2,1)S(1)}, u32[]{:S(2)}, u32[]{:S(2)}) collective-permute-start(bf16[608,128]{1,0:T(8,128)(2,1)} %get-tuple-element.258), channel_id=1, source_target_pairs={{0,3},{1,2},{2,1},{3,0},{4,7},{5,6},{6,5},{7,4},{8,11},{9,10},{10,... | collective-permute-start | bytes 466952 | tf_op jit(solution)/shard_map/ppermute | solution.py:463
  14.3 23.6 %collective-permute-start.12 = (bf16[608,128]{1,0:T(8,128)(2,1)}, bf16[608,128]{1,0:T(8,128)(2,1)S(1)}, u32[]{:S(2)}, u32[]{:S(2)}) collective-permute-start(bf16[608,128]{1,0:T(8,128)(2,1)} %get-tuple-element.259), channel_id=1, source_target_pairs={{0,4},{1,5},{2,6},{3,7},{4,0},{5,1},{6,2},{7,3},{8,12},{9,13},{10,... | collective-permute-start | bytes 466952 | tf_op jit(solution)/shard_map/ppermute | solution.py:463
  16.0 21.9 %collective-permute-start.13 = (bf16[608,128]{1,0:T(8,128)(2,1)}, bf16[608,128]{1,0:T(8,128)(2,1)S(1)}, u32[]{:S(2)}, u32[]{:S(2)}) collective-permute-start(bf16[608,128]{1,0:T(8,128)(2,1)} %get-tuple-element.260), channel_id=1, source_target_pairs={{0,5},{1,4},{2,7},{3,6},{4,1},{5,0},{6,3},{7,2},{8,13},{9,12},{10,... | collective-permute-start | bytes 466952 | tf_op jit(solution)/shard_map/ppermute | solution.py:463
  16.1 28.0 %collective-permute-start.14 = (bf16[608,128]{1,0:T(8,128)(2,1)S(1)}, bf16[608,128]{1,0:T(8,128)(2,1)S(1)}, u32[]{:S(2)}, u32[]{:S(2)}) collective-permute-start(bf16[608,128]{1,0:T(8,128)(2,1)S(1)} %copy-done.6), channel_id=1, source_target_pairs={{0,6},{1,7},{2,4},{3,5},{4,2},{5,3},{6,0},{7,1},{8,14},{9,15},{10,... | collective-permute-start | bytes 466952 | tf_op jit(solution)/shard_map/ppermute | solution.py:463
  31.0 15.8 %collective-permute-start.15 = (bf16[608,128]{1,0:T(8,128)(2,1)S(1)}, bf16[608,128]{1,0:T(8,128)(2,1)S(1)}, u32[]{:S(2)}, u32[]{:S(2)}) collective-permute-start(bf16[608,128]{1,0:T(8,128)(2,1)S(1)} %copy-done.5), channel_id=1, source_target_pairs={{0,7},{1,6},{2,5},{3,4},{4,3},{5,2},{6,1},{7,0},{8,15},{9,14},{10,... | collective-permute-start | bytes 466952 | tf_op jit(solution)/shard_map/ppermute | solution.py:463
  50.0 17.8 %collective-permute-start.16 = (bf16[264,512]{1,0:T(8,128)(2,1)}, bf16[264,512]{1,0:T(8,128)(2,1)}, u32[]{:S(2)}, u32[]{:S(2)}) collective-permute-start(bf16[264,512]{1,0:T(8,128)(2,1)} %get-tuple-element.264), channel_id=1, source_target_pairs={{0,8},{8,0},{16,24},{24,16},{1,9},{9,1},{17,25},{25,17},{2,10},{10... | collective-permute-start | bytes 811016 | tf_op jit(solution)/shard_map/ppermute | solution.py:482
  53.3 22.1 %collective-permute-start.17 = (bf16[264,512]{1,0:T(8,128)(2,1)}, bf16[264,512]{1,0:T(8,128)(2,1)}, u32[]{:S(2)}, u32[]{:S(2)}) collective-permute-start(bf16[264,512]{1,0:T(8,128)(2,1)} %get-tuple-element.265), channel_id=1, source_target_pairs={{0,16},{8,24},{16,0},{24,8},{1,17},{9,25},{17,1},{25,9},{2,18},{10... | collective-permute-start | bytes 811016 | tf_op jit(solution)/shard_map/ppermute | solution.py:482
  55.1 22.4 %collective-permute-start.18 = (bf16[264,512]{1,0:T(8,128)(2,1)S(1)}, bf16[264,512]{1,0:T(8,128)(2,1)}, u32[]{:S(2)}, u32[]{:S(2)}) collective-permute-start(bf16[264,512]{1,0:T(8,128)(2,1)S(1)} %get-tuple-element.267), channel_id=1, source_target_pairs={{0,24},{8,16},{16,8},{24,0},{1,25},{9,17},{17,9},{25,1},{2,26},{10... | collective-permute-start | bytes 811016 | tf_op jit(solution)/shard_map/ppermute | solution.py:482
  67.7 7.8 %copy-start.2 = (bf16[5,128,512]{2,1,0:T(8,128)(2,1)S(1)}, bf16[5,128,512]{2,1,0:T(8,128)(2,1)}, u32[]{:S(2)}) copy-start(bf16[5,128,512]{2,1,0:T(8,128)(2,1)} %constant_dynamic-slice_fusion.flux_ref) | copy-start | bytes 1966084
  67.7 7.8 %copy-start.4 = (bf16[264,512]{1,0:T(8,128)(2,1)S(1)}, bf16[264,512]{1,0:T(8,128)(2,1)}, u32[]{:S(2)}) copy-start(bf16[264,512]{1,0:T(8,128)(2,1)} %get-tuple-element.263.refs_0_) | copy-start | bytes 811012
  67.7 11.3 %copy-start.1 = (bf16[1792,512]{1,0:T(8,128)(2,1)S(1)}, bf16[1792,512]{1,0:T(8,128)(2,1)}, u32[]{:S(2)}) copy-start(bf16[1792,512]{1,0:T(8,128)(2,1)} %get-tuple-element.269) | copy-start | bytes 5505028
  67.7 11.3 %copy-start.3 = (bf16[328,512]{1,0:T(8,128)(2,1)S(1)}, bf16[328,512]{1,0:T(8,128)(2,1)}, u32[]{:S(2)}) copy-start(bf16[328,512]{1,0:T(8,128)(2,1)} %get-tuple-element.281) | copy-start | bytes 1007620
where the time goes:
time: 98.8 us; the launch traced here: 98.4 us
  waiting for transfers between devices  35.5 us (36%)
  Pallas kernels  24.8 us (25%)
  starting transfers between devices  19.7 us (20%)
  blocking collectives  13.9 us (14%)
  local copies, waits for them, and re-layouts  2.53 us (3%)
  between operations  1.6 us (2%)
    ppermute x7, waiting for transfers between devices, shards(): lax.ppermute(spills[d], 'obs', [(i, i ^ d) for i in range(columns)])  27.8 us
    all_to_all x1, blocking collectives, run(): sums = lax.all_to_all(sums, both, split_axis=0, concat_axis=0, tiled=True)  13.9 us
    ppermute x3, waiting for transfers between devices, swap(): lax.ppermute(arrays[n], 'flux', [(i, i ^ n) for i in range(owners)])  7.73 us
    all_to_all x1, starting transfers between devices, shards(): lax.all_to_all(send.reshape(devices, first_height, LANES), both, split_ax...  7.3 us
    pallas_call x2, Pallas kernels, regroup(): pl.pallas_call(functools.partial(regroup_kernel, sizes, start, count, hei...  7.27 us
    ppermute x7, starting transfers between devices, shards(): lax.ppermute(spills[d], 'obs', [(i, i ^ d) for i in range(columns)])  6.76 us
    ppermute x3, starting transfers between devices, swap(): lax.ppermute(arrays[n], 'flux', [(i, i ^ n) for i in range(owners)])  5.68 us
    pallas_call x1, Pallas kernels, run(): pl.pallas_call(functools.partial(adjoint_kernel, sizes, more), in_specs=[...  5.02 us
  transfers between devices with their start and end apart: 11, of which 5 were waited for; matrix products, arithmetic and copies ran while one was open for 3% of the time, Pallas kernels for 14%

commit v1 on v0

--- a/solution.py
+++ b/solution.py
@@ -536,31 +536,20 @@
     late_spills = lax.optimization_barrier((spills, early))[0]
     rests = list(regroup(late_spills, sizes.base, sizes.rest, sizes.rest_notes, "regroup_rest"))
 
-    def follow(more):
-        def run(rests):
-            height, results, before = sizes.rest_notes + more, rests[:1], ()
-            for n in range(1, owners):
-                rest = lax.optimization_barrier((rests[n][:height], before))[0]
-                before = lax.ppermute(rest, "flux", [(i, i ^ n) for i in range(owners)])
-                results.append(lax.dynamic_update_slice(rests[n], before, (0, 0)))
-            return results
-
-        return run if more else lambda rests: rests
-
     level = level[0, 0]
-    rests = lax.switch(level, [follow(n) for n in sizes.levels], rests)
-
-    reads = []
-    sums = early[None]
-    for first, end in ((0, owners - 1), (owners - 1, owners)):
-        sums, read = forward_second(
-            own_flux, sums, bases[first:end], first, sizes.base_notes, sizes.base, "forward_second"
-        )
-        reads.append(read)
-    kept = (feet_first, read_first, *reads)
+
+    sums, read_second = forward_second(
+        own_flux, early[None], bases[:-1], 0, sizes.base_notes, sizes.base, "forward_second"
+    )
+    kept = (feet_first, read_first, read_second)
 
     def finish(more):
         def run(own_flux, kept, sums, bases, rests, at):
+            if more:
+                rests = swap([rest[: sizes.rest_notes + more] for rest in rests])
+            sums, read_last = forward_second(
+                own_flux, sums, bases[-1:], owners - 1, sizes.base_notes, sizes.base, "forward_last"
+            )
             if more:
                 sums, read_more = forward_second(
                     own_flux, sums, rests, 0, sizes.rest_notes, more, "forward_more"
@@ -586,7 +575,7 @@
                 ],
                 compiler_params=params,
                 name="adjoint",
-            )(at, sums, *kept, *bases, *rests)
+            )(at, sums, *kept, read_last, *bases, *rests)
 
         return run
 

time: 98.8 us -> 98.7 us (level)
  waiting for transfers between devices: 35.5 us -> 37.2 us
  Pallas kernels: 24.8 us -> 23.1 us
    ppermute x3, waiting for transfers between devices: 7.73 us -> 9.42 us  [swap(): lax.ppermute(arrays[n], 'flux', [(i, i ^ n) for i in range(owners)])]
  transfers between devices with their start and end apart: 11 -> 11, of which waited for: 5 -> 6; matrix products, arithmetic and copies ran while one was open for 3% -> 3% of each run, Pallas kernels for 14% -> 13%
where the time goes in v1:
time: 98.7 us; the launch traced here: 98.3 us
  waiting for transfers between devices  37.2 us (38%)
  Pallas kernels  23.1 us (23%)
  starting transfers between devices  19.7 us (20%)
  blocking collectives  13.9 us (14%)
  local copies, waits for them, and re-layouts  2.57 us (3%)
  between operations  1.55 us (2%)
    ppermute x7, waiting for transfers between devices, shards(): lax.ppermute(spills[d], 'obs', [(i, i ^ d) for i in range(columns)])  27.8 us
    all_to_all x1, blocking collectives, run(): sums = lax.all_to_all(sums, both, split_axis=0, concat_axis=0, tiled=True)  13.9 us
    ppermute x3, waiting for transfers between devices, swap(): lax.ppermute(arrays[n], 'flux', [(i, i ^ n) for i in range(owners)])  9.42 us
    all_to_all x1, starting transfers between devices, shards(): lax.all_to_all(send.reshape(devices, first_height, LANES), both, split_ax...  7.3 us
    ppermute x7, starting transfers between devices, shards(): lax.ppermute(spills[d], 'obs', [(i, i ^ d) for i in range(columns)])  6.76 us
    pallas_call x2, Pallas kernels, regroup(): pl.pallas_call(functools.partial(regroup_kernel, sizes, start, count, hei...  6.49 us
    ppermute x3, starting transfers between devices, swap(): lax.ppermute(arrays[n], 'flux', [(i, i ^ n) for i in range(owners)])  5.68 us
    pallas_call x1, Pallas kernels, run(): pl.pallas_call(functools.partial(adjoint_kernel, sizes, more), in_specs=[...  5.01 us
  transfers between devices with their start and end apart: 11, of which 6 were waited for; matrix products, arithmetic and copies ran while one was open for 3% of the time, Pallas kernels for 13%

profile of v1, /device:TPU:0, one launch (start us, length us, event | category | flops | bytes accessed | tf_op | source)
XLA Modules:
  0.0 98.3 jit_solution(10043673681517901447)
XLA Ops:
  0.6 0.1 pad_add_fusion.at_ref
  0.7 4.2 %pack.1 = (bf16[4,8,232,128]{3,2,1,0:T(8,128)(2,1)}, bf16[608,128]{1,0:T(8,128)(2,1)}, bf16[608,128]{1,0:T(8,128)(2,1)}, bf16[608,128]{1,0:T(8,128)(2,1)}, bf16[...) custom-call(s32[3]{0:T(128)S(1)} %pad_add_fusion.at_ref, ...), custom_call_target="tpu_custom_call" | custom-call | tf_op jit(solution)/shard_map/pack/pallas_call | solution.py:433
  4.9 0.0 copy-start.12
  4.9 0.0 copy-start.11
  4.9 0.0 copy-start.10
  4.9 0.0 copy-start.9
  4.9 0.0 copy-start
  5.0 7.3 %all-to-all-start.4 = ((bf16[32,232,128]{2,1,0:T(8,128)(2,1)}), bf16[32,232,128]{2,1,0:T(8,128)(2,1)S(1)}, u32[]{:S(2)}, u32[]{:S(2)}) async-start(bf16[32,232,128]{2,1,0:T(8,128)(2,1)} %bitcast.18), calls=%async_computation.4 | async-start | bytes 3801088 | tf_op jit(solution)/shard_map/all_to_all | solution.py:458
  12.3 0.0 copy-done.12
  12.3 0.3 collective-permute-start.9
  12.6 0.0 copy-done.11
  12.6 1.7 %collective-permute-start.10 = (bf16[608,128]{1,0:T(8,128)(2,1)S(1)}, bf16[608,128]{1,0:T(8,128)(2,1)S(1)}, u32[]{:S(2)}, u32[]{:S(2)}) collective-permute-start(bf16[608,128]{1,0:T(8,128)(2,1)S(1)} %copy-done.11), channel_id=1, source_target_pairs={{0,2},{1,3},{2,0},{3,1},{4,6},{5,7},{6,4},{7,5},{8,10},{9,11},{10,... | collective-permute-start | bytes 466952 | tf_op jit(solution)/shard_map/ppermute | solution.py:463
  14.3 0.0 collective-permute-start.11
  14.3 1.7 %collective-permute-start.12 = (bf16[608,128]{1,0:T(8,128)(2,1)}, bf16[608,128]{1,0:T(8,128)(2,1)S(1)}, u32[]{:S(2)}, u32[]{:S(2)}) collective-permute-start(bf16[608,128]{1,0:T(8,128)(2,1)} %get-tuple-element.214), channel_id=1, source_target_pairs={{0,4},{1,5},{2,6},{3,7},{4,0},{5,1},{6,2},{7,3},{8,12},{9,13},{10,... | collective-permute-start | bytes 466952 | tf_op jit(solution)/shard_map/ppermute | solution.py:463
  16.0 0.1 collective-permute-start.13
  16.1 0.0 collective-permute-done.9.refs_1_
  16.1 0.0 copy-done.10
  16.1 2.6 %collective-permute-start.14 = (bf16[608,128]{1,0:T(8,128)(2,1)S(1)}, bf16[608,128]{1,0:T(8,128)(2,1)S(1)}, u32[]{:S(2)}, u32[]{:S(2)}) collective-permute-start(bf16[608,128]{1,0:T(8,128)(2,1)S(1)} %copy-done.10), channel_id=1, source_target_pairs={{0,6},{1,7},{2,4},{3,5},{4,2},{5,3},{6,0},{7,1},{8,14},{9,15},{10,... | collective-permute-start | bytes 466952 | tf_op jit(solution)/shard_map/ppermute | solution.py:463
  18.7 12.4 %collective-permute-done.10.refs_2_ = bf16[608,128]{1,0:T(8,128)(2,1)S(1)} collective-permute-done((bf16[608,128]{1,0:T(8,128)(2,1)S(1)}, bf16[608,128]{1,0:T(8,128)(2,1)S(1)}, u32[]{:S(2)}, u32[]{:S(2)}) %collective-permute-start.10) | collective-permute-done | bytes 155680 | tf_op jit(solution)/shard_map/ppermute | solution.py:463
  31.1 0.0 copy-done.9
  31.1 0.4 collective-permute-start.15
  31.4 6.4 %collective-permute-done.11.refs_3_ = bf16[608,128]{1,0:T(8,128)(2,1)S(1)} collective-permute-done((bf16[608,128]{1,0:T(8,128)(2,1)}, bf16[608,128]{1,0:T(8,128)(2,1)S(1)}, u32[]{:S(2)}, u32[]{:S(2)}) %collective-permute-start.11) | collective-permute-done | bytes 155680 | tf_op jit(solution)/shard_map/ppermute | solution.py:463
  37.8 0.0 collective-permute-done.12.refs_4_
  37.8 0.0 collective-permute-done.13.refs_5_
  37.8 6.3 %collective-permute-done.14.refs_6_ = bf16[608,128]{1,0:T(8,128)(2,1)S(1)} collective-permute-done((bf16[608,128]{1,0:T(8,128)(2,1)S(1)}, bf16[608,128]{1,0:T(8,128)(2,1)S(1)}, u32[]{:S(2)}, u32[]{:S(2)}) %collective-permute-start.14) | collective-permute-done | bytes 155680 | tf_op jit(solution)/shard_map/ppermute | solution.py:463
  44.1 2.7 %collective-permute-done.15.refs_7_ = bf16[608,128]{1,0:T(8,128)(2,1)S(1)} collective-permute-done((bf16[608,128]{1,0:T(8,128)(2,1)S(1)}, bf16[608,128]{1,0:T(8,128)(2,1)S(1)}, u32[]{:S(2)}, u32[]{:S(2)}) %collective-permute-start.15) | collective-permute-done | bytes 155680 | tf_op jit(solution)/shard_map/ppermute | solution.py:463
  46.8 0.0 copy-done
  46.8 3.1 %regroup.1 = (bf16[264,512]{1,0:T(8,128)(2,1)}, bf16[264,512]{1,0:T(8,128)(2,1)}, bf16[264,512]{1,0:T(8,128)(2,1)}, bf16[264,512]{1,0:T(8,128)(2,1)S(1)}) custom-call(s32[3]{0:T(128)S(1)} %pad_add_fusion.at_ref, bf16[608,128]{1,0:T(8,128)(2,1)S(1)} %copy-done, bf16[608,128]{1,0:T(8,128)(2,1)S(1)} %collective-permute-done.9.refs_1_, ...), custom_call_target="tpu_custom_call" | custom-call | tf_op jit(solution)/shard_map/regroup/pallas_call | solution.py:470
  50.0 3.3 %collective-permute-start.16 = (bf16[264,512]{1,0:T(8,128)(2,1)}, bf16[264,512]{1,0:T(8,128)(2,1)}, u32[]{:S(2)}, u32[]{:S(2)}) collective-permute-start(bf16[264,512]{1,0:T(8,128)(2,1)} %get-tuple-element.219), channel_id=1, source_target_pairs={{0,8},{8,0},{16,24},{24,16},{1,9},{9,1},{17,25},{25,17},{2,10},{10... | collective-permute-start | bytes 811016 | tf_op jit(solution)/shard_map/ppermute | solution.py:482
  53.3 1.8 %collective-permute-start.17 = (bf16[264,512]{1,0:T(8,128)(2,1)}, bf16[264,512]{1,0:T(8,128)(2,1)}, u32[]{:S(2)}, u32[]{:S(2)}) collective-permute-start(bf16[264,512]{1,0:T(8,128)(2,1)} %get-tuple-element.220), channel_id=1, source_target_pairs={{0,16},{8,24},{16,0},{24,8},{1,17},{9,25},{17,1},{25,9},{2,18},{10... | collective-permute-start | bytes 811016 | tf_op jit(solution)/shard_map/ppermute | solution.py:482
  55.1 0.6 collective-permute-start.18
  55.6 2.0 %constant_dynamic-slice_fusion.flux_ref = bf16[5,128,512]{2,1,0:T(8,128)(2,1)} fusion(bf16[5,128,4096]{2,1,0:T(8,128)(2,1)} %bitcast.15, s32[]{:T(128)S(6)} %select_n.3), kind=kLoop, calls=%fused_computation.1 | loop fusion | bytes 1310724 | tf_op jit(solution)/shard_map/dynamic_slice | solution.py:521
  57.6 0.0 all-to-all-done.4.got_ref.all_ref
  57.6 0.0 copy-start.1
  57.6 0.0 copy-start.8
  57.6 3.8 %forward_first.1 = (f32[8,128]{1,0:T(8,128)S(1)}, s32[8,128]{1,0:T(8,128)S(1)}, bf16[1792,512]{1,0:T(8,128)(2,1)S(1)}, f32[8,1792]{1,0:T(8,128)S(1)}) custom-call(s32[3]{0:T(128)S(1)} %pad_add_fusion.at_ref, bf16[5,128,4096]{2,1,0:T(8,128)(2,1)} %bitcast.16, bf16[32,232,128]{2,1,0:T(8,128)(2,1)S(1)} %all-to-all-done.4.got_ref.all_ref, ...), custom_call_target="tpu_custom_call" | custom-call | tf_op jit(solution)/shard_map/forward_first/pallas_call | solution.py:493
  61.4 0.6 slice.27
  62.7 3.3 %regroup_rest.1 = (bf16[328,512]{1,0:T(8,128)(2,1)S(1)}, bf16[328,512]{1,0:T(8,128)(2,1)S(1)}, bf16[328,512]{1,0:T(8,128)(2,1)S(1)}, bf16[328,512]{1,0:T(8,128)(2,1)S(1)}) custom-call(s32[3]{0:T(128)S(1)} %pad_add_fusion.at_ref, bf16[608,128]{1,0:T(8,128)(2,1)S(1)} %copy-done, bf16[608,128]{1,0:T(8,128)(2,1)S(1)} %collective-permute-done.9.refs_1_, ...), custom_call_target="tpu_custom_call" | custom-call | tf_op jit(solution)/shard_map/regroup_rest/pallas_call | solution.py:470
  66.0 1.7 %collective-permute-done.16.refs_1_ = bf16[264,512]{1,0:T(8,128)(2,1)} collective-permute-done((bf16[264,512]{1,0:T(8,128)(2,1)}, bf16[264,512]{1,0:T(8,128)(2,1)}, u32[]{:S(2)}, u32[]{:S(2)}) %collective-permute-start.16) | collective-permute-done | bytes 270368 | tf_op jit(solution)/shard_map/ppermute | solution.py:482
  67.8 7.7 %collective-permute-done.17.refs_2_ = bf16[264,512]{1,0:T(8,128)(2,1)} collective-permute-done((bf16[264,512]{1,0:T(8,128)(2,1)}, bf16[264,512]{1,0:T(8,128)(2,1)}, u32[]{:S(2)}, u32[]{:S(2)}) %collective-permute-start.17) | collective-permute-done | bytes 270368 | tf_op jit(solution)/shard_map/ppermute | solution.py:482
  75.4 0.0 copy-done.1
  75.4 0.0 copy-done.8
  75.4 2.0 %forward_second.1 = (f32[32,8,128]{2,1,0:T(8,128)S(1)}, f32[8,768]{1,0:T(8,128)S(1)}) custom-call(s32[3]{0:T(128)S(1)} %pad_add_fusion.at_ref, bf16[5,128,512]{2,1,0:T(8,128)(2,1)S(1)} %copy-done.1, f32[1,8,128]{2,1,0:T(8,128)S(1)} %bitcast.14, bf16[264,512]{1,0:T(8,128)(2,1)S(1)} %copy-done.8, bf16[264,512]{1,0:T(8,128)(2,1)} %collective-permute-done.16.refs_1_, ...), custom_call_target="tpu_custom_call" | custom-call | tf_op jit(solution)/shard_map/forward_second/pallas_call | solution.py:524
  77.4 0.0 collective-permute-done.18
  77.5 20.7 %conditional.1 = ((f32[4,8]{1,0:T(4,128)}, f32[5,128,512]{2,1,0:T(8,128)})) conditional(s32[]{:T(128)} %bitcast.10, (s32[3]{0:T(128)S(1)}, bf16[5,128,512]{2,1,0:T(8,128)(2,1)S(1)}, f32[32,8,128]{2,1,0:T(8,128)S(1)}, bf16[264,512]{1,0:T(8,128)(2,1)}, bf16[1792,512]{1,0:T(8,128)(2,1)S(1)}, ...), branch_computations={%region_0.0_spmd, %region_1.0_spmd, %region_2.0_spmd, %region_3.0_... | conditional | bytes 21594324 | solution.py:582
  77.5 1.6 %forward_last.4 = (f32[32,8,128]{2,1,0:T(8,128)S(1)}, f32[8,256]{1,0:T(8,128)S(1)}) custom-call(s32[3]{0:T(128)S(1)} %get-tuple-element.104.at_ref, bf16[5,128,512]{2,1,0:T(8,128)(2,1)S(1)} %get-tuple-element.105.flux_ref, f32[32,8,128]{2,1,0:T(8,128)S(1)} %get-tuple-element.106.before_ref, bf16[264,512]{1,0:T(8,128)(2,1)} %get-tuple-element.107.refs_0_.refs_3_), custom_call_target="tpu_custom_call" | custom-call | tf_op jit(solution)/shard_map/cond/branch_0_fun/forward_last/pallas_call | solution.py:524
  79.0 13.9 %all_to_all.21.sums_ref = f32[32,8,128]{2,1,0:T(8,128)S(1)} all-to-all(f32[32,8,128]{2,1,0:T(8,128)S(1)} %get-tuple-element.108), channel_id=1, replica_groups=mesh['flux'=4,'obs'=8] {'flux','obs'}, dimensions={0} | all-to-all | bytes 262144 | tf_op jit(solution)/shard_map/cond/branch_0_fun/all_to_all | solution.py:561
  92.9 5.0 %adjoint.4 = (f32[4,8]{1,0:T(4,128)}, f32[5,128,512]{2,1,0:T(8,128)}) custom-call(s32[3]{0:T(128)S(1)} %get-tuple-element.104.at_ref, f32[32,8,128]{2,1,0:T(8,128)S(1)} %all_to_all.21.sums_ref, bf16[1792,512]{1,0:T(8,128)(2,1)S(1)} %get-tuple-element.109.feet_ref, f32[8,1792]{1,0:T(8,128)S(1)} %get-tuple-element.110.read_ref, ...), custom_call_target="tpu_custom_call" | custom-call | tf_op jit(solution)/shard_map/cond/branch_0_fun/adjoint/pallas_call | solution.py:564
Async XLA Ops:
  4.9 7.4 %copy-start.12 = (bf16[608,128]{1,0:T(8,128)(2,1)S(1)}, bf16[608,128]{1,0:T(8,128)(2,1)}, u32[]{:S(2)}) copy-start(bf16[608,128]{1,0:T(8,128)(2,1)} %get-tuple-element.211) | copy-start | bytes 466948
  4.9 7.7 %copy-start.11 = (bf16[608,128]{1,0:T(8,128)(2,1)S(1)}, bf16[608,128]{1,0:T(8,128)(2,1)}, u32[]{:S(2)}) copy-start(bf16[608,128]{1,0:T(8,128)(2,1)} %get-tuple-element.212) | copy-start | bytes 466948
  4.9 11.2 %copy-start.10 = (bf16[608,128]{1,0:T(8,128)(2,1)S(1)}, bf16[608,128]{1,0:T(8,128)(2,1)}, u32[]{:S(2)}) copy-start(bf16[608,128]{1,0:T(8,128)(2,1)} %get-tuple-element.216) | copy-start | bytes 466948
  4.9 26.1 %copy-start.9 = (bf16[608,128]{1,0:T(8,128)(2,1)S(1)}, bf16[608,128]{1,0:T(8,128)(2,1)}, u32[]{:S(2)}) copy-start(bf16[608,128]{1,0:T(8,128)(2,1)} %get-tuple-element.217) | copy-start | bytes 466948
  4.9 41.9 %copy-start = (bf16[608,128]{1,0:T(8,128)(2,1)S(1)}, bf16[608,128]{1,0:T(8,128)(2,1)}, u32[]{:S(2)}) copy-start(bf16[608,128]{1,0:T(8,128)(2,1)} %get-tuple-element.226.refs_0_) | copy-start | bytes 466948
  5.0 52.7 %all-to-all-start.4 = ((bf16[32,232,128]{2,1,0:T(8,128)(2,1)}), bf16[32,232,128]{2,1,0:T(8,128)(2,1)S(1)}, u32[]{:S(2)}, u32[]{:S(2)}) async-start(bf16[32,232,128]{2,1,0:T(8,128)(2,1)} %bitcast.18), calls=%async_computation.4 | async-start | bytes 3801088 | tf_op jit(solution)/shard_map/all_to_all | solution.py:458
  12.3 3.8 %collective-permute-start.9 = (bf16[608,128]{1,0:T(8,128)(2,1)S(1)}, bf16[608,128]{1,0:T(8,128)(2,1)S(1)}, u32[]{:S(2)}, u32[]{:S(2)}) collective-permute-start(bf16[608,128]{1,0:T(8,128)(2,1)S(1)} %copy-done.12), channel_id=1, source_target_pairs={{0,1},{1,0},{2,3},{3,2},{4,5},{5,4},{6,7},{7,6},{8,9},{9,8},{10,11... | collective-permute-start | bytes 466952 | tf_op jit(solution)/shard_map/ppermute | solution.py:463
  12.6 18.5 %collective-permute-start.10 = (bf16[608,128]{1,0:T(8,128)(2,1)S(1)}, bf16[608,128]{1,0:T(8,128)(2,1)S(1)}, u32[]{:S(2)}, u32[]{:S(2)}) collective-permute-start(bf16[608,128]{1,0:T(8,128)(2,1)S(1)} %copy-done.11), channel_id=1, source_target_pairs={{0,2},{1,3},{2,0},{3,1},{4,6},{5,7},{6,4},{7,5},{8,10},{9,11},{10,... | collective-permute-start | bytes 466952 | tf_op jit(solution)/shard_map/ppermute | solution.py:463
  14.3 23.6 %collective-permute-start.11 = (bf16[608,128]{1,0:T(8,128)(2,1)}, bf16[608,128]{1,0:T(8,128)(2,1)S(1)}, u32[]{:S(2)}, u32[]{:S(2)}) collective-permute-start(bf16[608,128]{1,0:T(8,128)(2,1)} %get-tuple-element.213), channel_id=1, source_target_pairs={{0,3},{1,2},{2,1},{3,0},{4,7},{5,6},{6,5},{7,4},{8,11},{9,10},{10,... | collective-permute-start | bytes 466952 | tf_op jit(solution)/shard_map/ppermute | solution.py:463
  14.3 23.6 %collective-permute-start.12 = (bf16[608,128]{1,0:T(8,128)(2,1)}, bf16[608,128]{1,0:T(8,128)(2,1)S(1)}, u32[]{:S(2)}, u32[]{:S(2)}) collective-permute-start(bf16[608,128]{1,0:T(8,128)(2,1)} %get-tuple-element.214), channel_id=1, source_target_pairs={{0,4},{1,5},{2,6},{3,7},{4,0},{5,1},{6,2},{7,3},{8,12},{9,13},{10,... | collective-permute-start | bytes 466952 | tf_op jit(solution)/shard_map/ppermute | solution.py:463
  16.0 21.9 %collective-permute-start.13 = (bf16[608,128]{1,0:T(8,128)(2,1)}, bf16[608,128]{1,0:T(8,128)(2,1)S(1)}, u32[]{:S(2)}, u32[]{:S(2)}) collective-permute-start(bf16[608,128]{1,0:T(8,128)(2,1)} %get-tuple-element.215), channel_id=1, source_target_pairs={{0,5},{1,4},{2,7},{3,6},{4,1},{5,0},{6,3},{7,2},{8,13},{9,12},{10,... | collective-permute-start | bytes 466952 | tf_op jit(solution)/shard_map/ppermute | solution.py:463
  16.1 28.0 %collective-permute-start.14 = (bf16[608,128]{1,0:T(8,128)(2,1)S(1)}, bf16[608,128]{1,0:T(8,128)(2,1)S(1)}, u32[]{:S(2)}, u32[]{:S(2)}) collective-permute-start(bf16[608,128]{1,0:T(8,128)(2,1)S(1)} %copy-done.10), channel_id=1, source_target_pairs={{0,6},{1,7},{2,4},{3,5},{4,2},{5,3},{6,0},{7,1},{8,14},{9,15},{10,... | collective-permute-start | bytes 466952 | tf_op jit(solution)/shard_map/ppermute | solution.py:463
  31.1 15.8 %collective-permute-start.15 = (bf16[608,128]{1,0:T(8,128)(2,1)S(1)}, bf16[608,128]{1,0:T(8,128)(2,1)S(1)}, u32[]{:S(2)}, u32[]{:S(2)}) collective-permute-start(bf16[608,128]{1,0:T(8,128)(2,1)S(1)} %copy-done.9), channel_id=1, source_target_pairs={{0,7},{1,6},{2,5},{3,4},{4,3},{5,2},{6,1},{7,0},{8,15},{9,14},{10,... | collective-permute-start | bytes 466952 | tf_op jit(solution)/shard_map/ppermute | solution.py:463
  50.0 17.8 %collective-permute-start.16 = (bf16[264,512]{1,0:T(8,128)(2,1)}, bf16[264,512]{1,0:T(8,128)(2,1)}, u32[]{:S(2)}, u32[]{:S(2)}) collective-permute-start(bf16[264,512]{1,0:T(8,128)(2,1)} %get-tuple-element.219), channel_id=1, source_target_pairs={{0,8},{8,0},{16,24},{24,16},{1,9},{9,1},{17,25},{25,17},{2,10},{10... | collective-permute-start | bytes 811016 | tf_op jit(solution)/shard_map/ppermute | solution.py:482
  53.3 22.1 %collective-permute-start.17 = (bf16[264,512]{1,0:T(8,128)(2,1)}, bf16[264,512]{1,0:T(8,128)(2,1)}, u32[]{:S(2)}, u32[]{:S(2)}) collective-permute-start(bf16[264,512]{1,0:T(8,128)(2,1)} %get-tuple-element.220), channel_id=1, source_target_pairs={{0,16},{8,24},{16,0},{24,8},{1,17},{9,25},{17,1},{25,9},{2,18},{10... | collective-permute-start | bytes 811016 | tf_op jit(solution)/shard_map/ppermute | solution.py:482
  55.1 22.4 %collective-permute-start.18 = (bf16[264,512]{1,0:T(8,128)(2,1)S(1)}, bf16[264,512]{1,0:T(8,128)(2,1)}, u32[]{:S(2)}, u32[]{:S(2)}) collective-permute-start(bf16[264,512]{1,0:T(8,128)(2,1)S(1)} %get-tuple-element.222), channel_id=1, source_target_pairs={{0,24},{8,16},{16,8},{24,0},{1,25},{9,17},{17,9},{25,1},{2,26},{10... | collective-permute-start | bytes 811016 | tf_op jit(solution)/shard_map/ppermute | solution.py:482
  57.6 17.8 %copy-start.1 = (bf16[5,128,512]{2,1,0:T(8,128)(2,1)S(1)}, bf16[5,128,512]{2,1,0:T(8,128)(2,1)}, u32[]{:S(2)}) copy-start(bf16[5,128,512]{2,1,0:T(8,128)(2,1)} %constant_dynamic-slice_fusion.flux_ref) | copy-start | bytes 1966084
  57.6 17.8 %copy-start.8 = (bf16[264,512]{1,0:T(8,128)(2,1)S(1)}, bf16[264,512]{1,0:T(8,128)(2,1)}, u32[]{:S(2)}) copy-start(bf16[264,512]{1,0:T(8,128)(2,1)} %get-tuple-element.218.refs_0_) | copy-start | bytes 811012
